TPU v7x, 32 devices: a whole 2x2x4 slice. The times are simulated.
32 devices in a mesh: depth: 4 (over x, core), row: 2 (over y), col: 4 (over z).
Axes of the slice: x: 2, y: 2, z: 4, core: 2. Of those that a mesh axis runs over, the one named last changes fastest.
Arguments:
- tokens: bfloat16 [96, 8192], P(('depth', 'row')), may hold values from -6 to 6
- out_grad: bfloat16 [96, 8192], P(('depth', 'row')), may hold values from -0.59765625 to 0.59765625
- gate_weight: bfloat16 [8192, 16384], P('depth', ('row', 'col')), may hold values from -0.0625 to 0.0625
- up_weight: bfloat16 [8192, 16384], P('depth', ('row', 'col')), may hold values from -0.0625 to 0.0625
- down_weight: bfloat16 [16384, 8192], P(('row', 'col'), 'depth'), may hold values from -0.046875 to 0.046875
Outputs:
- input_grad: bfloat16 [96, 8192], P(('depth', 'row', 'col'))
- gate_grad: bfloat16 [8192, 16384], P('depth', ('row', 'col'))
- up_grad: bfloat16 [8192, 16384], P('depth', ('row', 'col'))
- down_grad: bfloat16 [16384, 8192], P(('row', 'col'), 'depth')
All inputs are finite; a program needn't handle non-finite values.
Results may differ from a plain program's by a relative error of at most 0.024.
Values may be sent and summed in bfloat16 or wider, within the bound.
A program may use at most 320 MiB of HBM per device.

v0:
```python
import jax
import jax.numpy as jnp
from jax import lax
from jax.sharding import PartitionSpec as P


def contract_rows(left, right):
    return lax.dot_general(
        left, right, (((0,), (0,)), ((), ())), preferred_element_type=jnp.float32
    )


def contract_cols(left, right):
    return lax.dot_general(
        left, right, (((1,), (1,)), ((), ())), preferred_element_type=jnp.float32
    )


def swiglu_terms(gate, up, hidden_grad):
    sig = jax.nn.sigmoid(gate)
    act = gate * sig
    hidden = (act * up).astype(jnp.bfloat16)
    gate_term = (hidden_grad * up * sig * (1.0 + gate * (1.0 - sig))).astype(jnp.bfloat16)
    up_term = (hidden_grad * act).astype(jnp.bfloat16)
    return (hidden, gate_term, up_term)


def block_work(tok_part, grad_part, gate_full, up_full, down_full):
    gate = jnp.dot(tok_part, gate_full, preferred_element_type=jnp.float32)
    up = jnp.dot(tok_part, up_full, preferred_element_type=jnp.float32)
    hidden_grad = contract_cols(grad_part, down_full)
    hidden, gate_term, up_term = swiglu_terms(gate, up, hidden_grad)
    partial_in = contract_cols(gate_term, gate_full) + contract_cols(up_term, up_full)
    return (hidden, gate_term, up_term, partial_in)


def on_device(tokens, out_grad, gate_weight, up_weight, down_weight):
    gate_full, up_full, down_full = (
        lax.all_gather(gate_weight, "depth", axis=0, tiled=True),
        lax.all_gather(up_weight, "depth", axis=0, tiled=True),
        lax.all_gather(down_weight, "depth", axis=1, tiled=True),
    )
    all_tok, all_grad = (
        lax.all_gather(tokens, "row", axis=0, tiled=True),
        lax.all_gather(out_grad, "row", axis=0, tiled=True),
    )
    hidden, gate_term, up_term, partial_in = block_work(
        all_tok, all_grad, gate_full, up_full, down_full
    )
    input_grad = lax.psum_scatter(
        partial_in, ("row", "col"), scatter_dimension=0, tiled=True
    ).astype(jnp.bfloat16)
    gate_grad, up_grad, down_grad = (
        lax.psum_scatter(
            contract_rows(all_tok, gate_term).astype(jnp.bfloat16),
            "depth",
            scatter_dimension=0,
            tiled=True,
        ).astype(jnp.float32),
        lax.psum_scatter(
            contract_rows(all_tok, up_term).astype(jnp.bfloat16),
            "depth",
            scatter_dimension=0,
            tiled=True,
        ).astype(jnp.float32),
        lax.psum_scatter(
            contract_rows(hidden, all_grad).astype(jnp.bfloat16),
            "depth",
            scatter_dimension=1,
            tiled=True,
        ).astype(jnp.float32),
    )
    return (
        input_grad,
        gate_grad.astype(jnp.bfloat16),
        up_grad.astype(jnp.bfloat16),
        down_grad.astype(jnp.bfloat16),
    )


def solution(mesh):
    return jax.shard_map(
        on_device,
        mesh=mesh,
        in_specs=(
            P(("depth", "row"), None),
            P(("depth", "row"), None),
            P("depth", ("row", "col")),
            P("depth", ("row", "col")),
            P(("row", "col"), "depth"),
        ),
        out_specs=(
            P(("depth", "row", "col"), None),
            P("depth", ("row", "col")),
            P("depth", ("row", "col")),
            P(("row", "col"), "depth"),
        ),
        check_vma=False,
    )
```

profile of v0, /device:TPU:0, one launch (start us, length us, event | category | flops | bytes accessed | tf_op | source)
XLA Modules:
  0.0 1366.0 jit_solution(4740683361323625452)
XLA Ops:
  7.2 0.0 all-gather.8.cloned.1.call-start
  7.2 0.7 all-gather.8.cloned.1.call-update
  7.9 0.0 all-gather.10.cloned.1.call-start
  7.9 0.7 all-gather.10.cloned.1.call-update
  8.6 0.0 all-gather.6.cloned.1.call-start
  8.7 0.7 all-gather.6.cloned.1.call-update
  9.4 0.0 reduce-scatter.4.cloned.1.call-start
  9.4 10.2 all-gather.1
  19.6 0.1 reshape.11
  19.7 8.4 all-gather
  28.1 0.1 reshape.9
  28.2 185.6 %all-gather.8.cloned.1.call-done = bf16[8192,2048]{1,0:T(8,128)(2,1)} async-done(((bf16[2048,2048]{1,0:T(8,128)(2,1)}), bf16[8192,2048]{1,0:T(8,128)(2,1)}) %all-gather.8.cloned.1.call-update) | async-done | bytes 33554448 | tf_op jit(solution)/shard_map/all_gather | solution.py:40
  213.8 15.9 %fusion.3 = f32[24,2048]{1,0:T(8,128)S(1)} fusion(bf16[24,8192]{1,0:T(8,128)(2,1)S(1)} %reshape.11, bf16[8192,2048]{1,0:T(8,128)(2,1)} %all-gather.8.cloned.1.call-done), kind=kOutput, calls=%fused_computation.11 | convolution fusion | flops 805306368 | bytes 34144256 | tf_op jit(solution)/shard_map/dot_general | solution.py:30
  229.7 187.2 %all-gather.10.cloned.1.call-done = bf16[8192,2048]{1,0:T(8,128)(2,1)} async-done(((bf16[2048,2048]{1,0:T(8,128)(2,1)}), bf16[8192,2048]{1,0:T(8,128)(2,1)}) %all-gather.10.cloned.1.call-update) | async-done | bytes 33554448 | tf_op jit(solution)/shard_map/all_gather | solution.py:39
  416.9 15.9 %fusion.4 = f32[24,2048]{1,0:T(8,128)S(1)} fusion(bf16[24,8192]{1,0:T(8,128)(2,1)S(1)} %reshape.11, bf16[8192,2048]{1,0:T(8,128)(2,1)} %all-gather.10.cloned.1.call-done), kind=kOutput, calls=%fused_computation.12 | convolution fusion | flops 805306368 | bytes 34144256 | tf_op jit(solution)/shard_map/dot_general | solution.py:29
  432.8 187.2 %all-gather.6.cloned.1.call-done = bf16[2048,8192]{1,0:T(8,128)(2,1)} async-done(((bf16[2048,2048]{1,0:T(8,128)(2,1)}), bf16[2048,8192]{1,0:T(8,128)(2,1)}) %all-gather.6.cloned.1.call-update) | async-done | bytes 33554448 | tf_op jit(solution)/shard_map/all_gather | solution.py:41
  620.1 14.6 %multiply_convert_fusion.1 = (bf16[24,2048]{1,0:T(8,128)(2,1)S(1)}, bf16[24,2048]{1,0:T(8,128)(2,1)S(1)}) fusion(f32[24,2048]{1,0:T(8,128)S(1)} %fusion.4, f32[24,2048]{1,0:T(8,128)S(1)} %fusion.3, bf16[24,8192]{1,0:T(8,128)(2,1)S(1)} %reshape.9, bf16[2048,8192]{1,0:T(8,128)(2,1)} %all-gather.6.cloned.1.call-done), kind=kOutput, calls=%fused_computation.5 | convolution fusion | flops 805945344 | bytes 34537472 | tf_op jit(solution)/shard_map/dot_general | solution.py:14
  634.7 13.9 %convert_bitcast_fusion.1 = bf16[8192,2048]{0,1:T(8,128)(2,1)} fusion(bf16[24,2048]{1,0:T(8,128)(2,1)S(1)} %get-tuple-element.17, bf16[24,8192]{1,0:T(8,128)(2,1)S(1)} %reshape.11), kind=kOutput, calls=%fused_computation.1 | convolution fusion | flops 822083584 | bytes 34045952 | tf_op jit(solution)/shard_map/dot_general | solution.py:8
  648.6 0.0 reduce-scatter.6.cloned.1.call-start
  648.7 19.6 %convert_bitcast_fusion = bf16[8192,2048]{0,1:T(8,128)(2,1)} fusion(bf16[24,2048]{1,0:T(8,128)(2,1)S(1)} %get-tuple-element.16, bf16[24,8192]{1,0:T(8,128)(2,1)S(1)} %reshape.11), kind=kOutput, calls=%fused_computation | convolution fusion | flops 822083584 | bytes 34045952 | tf_op jit(solution)/shard_map/dot_general | solution.py:8
  668.3 0.2 reduce-scatter.8.cloned.1.call-start
  668.6 22.0 %convolution_convert_fusion = bf16[2048,8192]{1,0:T(8,128)(2,1)} fusion(bf16[24,8192]{1,0:T(8,128)(2,1)S(1)} %reshape.9, f32[24,2048]{1,0:T(8,128)S(1)} %fusion.3, f32[24,2048]{1,0:T(8,128)S(1)} %fusion.4), kind=kOutput, calls=%fused_computation.2 | convolution fusion | flops 822378496 | bytes 34340864 | tf_op jit(solution)/shard_map/dot_general | solution.py:8
  690.6 0.6 dynamic-slice
  691.9 15.5 %fusion.5 = f32[24,8192]{1,0:T(8,128)S(1)} fusion(bf16[24,2048]{1,0:T(8,128)(2,1)S(1)} %get-tuple-element.17, bf16[8192,2048]{1,0:T(8,128)(2,1)} %all-gather.10.cloned.1.call-done), kind=kOutput, calls=%fused_computation.13 | convolution fusion | flops 805306368 | bytes 34439168 | tf_op jit(solution)/shard_map/dot_general | solution.py:14
  707.3 15.0 %convolution_add_fusion = f32[24,8192]{1,0:T(8,128)S(1)} fusion(f32[24,8192]{1,0:T(8,128)S(1)} %fusion.5, bf16[24,2048]{1,0:T(8,128)(2,1)S(1)} %get-tuple-element.16, bf16[8192,2048]{1,0:T(8,128)(2,1)} %all-gather.8.cloned.1.call-done), kind=kOutput, calls=%fused_computation.3 | convolution fusion | flops 805502976 | bytes 35225600 | tf_op jit(solution)/shard_map/dot_general | solution.py:14
  722.3 49.3 %all-reduce.2 = bf16[24,8192]{1,0:T(8,128)(2,1)S(1)} all-reduce(f32[24,8192]{1,0:T(8,128)S(1)} %convolution_add_fusion), channel_id=2, replica_groups=mesh['depth'=4,'row'=2,'col'=4] {'row','col'}, use_global_device_ids=true, to_apply=%region_0.0.clone | all-reduce | flops 196608 | bytes 1179648
  771.6 0.7 dynamic-slice_convert_fusion
  772.3 111.5 %reduce-scatter.4.cloned.1.call-done = bf16[2048,2048]{0,1:T(8,128)(2,1)} async-done(((bf16[8192,2048]{0,1:T(8,128)(2,1)}), bf16[2048,2048]{0,1:T(8,128)(2,1)}) %reduce-scatter.4.cloned.1.call-update) | async-done | bytes 8388624 | tf_op jit(solution)/shard_map/reduce_scatter | solution.py:54
  883.8 12.4 copy.13
  896.2 225.1 %reduce-scatter.6.cloned.1.call-done = bf16[2048,2048]{0,1:T(8,128)(2,1)} async-done(((bf16[8192,2048]{0,1:T(8,128)(2,1)}), bf16[2048,2048]{0,1:T(8,128)(2,1)}) %reduce-scatter.6.cloned.1.call-update) | async-done | bytes 8388624 | tf_op jit(solution)/shard_map/reduce_scatter | solution.py:60
  1121.3 12.4 copy.14
  1133.7 225.5 %reduce-scatter.8.cloned.1.call-done = bf16[2048,2048]{1,0:T(8,128)(2,1)} async-done(((bf16[2048,8192]{1,0:T(8,128)(2,1)}), bf16[2048,2048]{1,0:T(8,128)(2,1)}) %reduce-scatter.8.cloned.1.call-update) | async-done | bytes 8388624 | tf_op jit(solution)/shard_map/reduce_scatter | solution.py:66
  (5 shorter events, 0.1 us)
Async XLA Ops:
  7.2 206.7 %all-gather.8.cloned.1.call-start = ((), (), s32[]{:S(2)}) async-start(), calls=%async_computation.4 | async-start | bytes 41943040 | tf_op jit(solution)/shard_map/all_gather | solution.py:40
  7.9 409.0 %all-gather.10.cloned.1.call-start = ((), (), s32[]{:S(2)}) async-start(), calls=%async_computation.5 | async-start | bytes 41943040 | tf_op jit(solution)/shard_map/all_gather | solution.py:39
  8.6 611.4 %all-gather.6.cloned.1.call-start = ((), (), s32[]{:S(2)}) async-start(), calls=%async_computation.3 | async-start | bytes 41943040 | tf_op jit(solution)/shard_map/all_gather | solution.py:41
  9.4 874.4 %reduce-scatter.4.cloned.1.call-start = ((), (), s32[]{:S(2)}) async-start(), calls=%async_computation.6 | async-start | bytes 41943040 | tf_op jit(solution)/shard_map/reduce_scatter | solution.py:54
  648.6 472.6 %reduce-scatter.6.cloned.1.call-start = ((), (), s32[]{:S(2)}) async-start(), calls=%async_computation.7 | async-start | bytes 41943040 | tf_op jit(solution)/shard_map/reduce_scatter | solution.py:60
  668.3 22.3 %copy-start = (u32[32]{0:T(128)S(1)}, u32[32]{0:T(128)}, u32[]{:S(2)}) copy-start(u32[32]{0:T(128)} %constant.6) | copy-start | bytes 388
  668.3 690.8 %reduce-scatter.8.cloned.1.call-start = ((), (), s32[]{:S(2)}) async-start(), calls=%async_computation.8 | async-start | bytes 41943040 | tf_op jit(solution)/shard_map/reduce_scatter | solution.py:66
Sparse Core Ops, SparseCore 0:
  9.6 204.2 all-gather.7
  215.4 201.5 all-gather.9
  418.5 201.5 all-gather.5
  648.8 234.9 reduce-scatter.3
  886.2 234.9 reduce-scatter.5
  1124.3 234.8 reduce-scatter.7
where the time goes:
time: 1370 us
  waiting for transfers between devices  1120 us (82%)
  matrix products  132 us (10%)
  blocking collectives  67.9 us (5%)
  local copies, waits for them, and re-layouts  26.3 us (2%)
  between operations  14.8 us (1%)
    reduce_scatter x1, waiting for transfers between devices, on_device(): lax.psum_scatter(contract_rows(hidden, all_grad).astype(jnp.bfloat16), 'd...  225 us
    reduce_scatter x1, waiting for transfers between devices, on_device(): lax.psum_scatter(contract_rows(all_tok, up_term).astype(jnp.bfloat16), 'd...  225 us
    all_gather x1, waiting for transfers between devices, on_device(): lax.all_gather(down_weight, 'depth', axis=1, tiled=True)  187 us
    all_gather x1, waiting for transfers between devices, on_device(): lax.all_gather(gate_weight, 'depth', axis=0, tiled=True)  187 us
    all_gather x1, waiting for transfers between devices, on_device(): lax.all_gather(up_weight, 'depth', axis=0, tiled=True)  186 us
    reduce_scatter x1, waiting for transfers between devices, on_device(): lax.psum_scatter(contract_rows(all_tok, gate_term).astype(jnp.bfloat16),...  112 us
    dot_general x3, matrix products, contract_rows(): lax.dot_general(left, right, (((0,), (0,)), ((), ())), preferred_element_...  55.5 us
    unnamed x1, blocking collectives  49.3 us
  transfers between devices with their start and end apart: 6, of which 6 were waited for; matrix products, arithmetic and copies ran while one was open for 10% of the time, Pallas kernels for 0%

commit v1 on v0

v1 whole, which is shorter than its diff:
```python
import functools

import jax
import jax.numpy as jnp
import numpy as np
from jax import lax
from jax.experimental import pallas as pl
from jax.experimental.pallas import tpu as pltpu
from jax.sharding import PartitionSpec as P


def contract_rows(left, right):
    return lax.dot_general(
        left, right, (((0,), (0,)), ((), ())), preferred_element_type=jnp.float32
    )


def contract_cols(left, right):
    return lax.dot_general(
        left, right, (((1,), (1,)), ((), ())), preferred_element_type=jnp.float32
    )


def swiglu_terms(gate, up, hidden_grad):
    sig = jax.nn.sigmoid(gate)
    act = gate * sig
    hidden = (act * up).astype(jnp.bfloat16)
    gate_term = (hidden_grad * up * sig * (1.0 + gate * (1.0 - sig))).astype(jnp.bfloat16)
    up_term = (hidden_grad * act).astype(jnp.bfloat16)
    return (hidden, gate_term, up_term)


def weight_stationary(n_depth, n_row, n_col):
    def on_device(tokens, out_grad, gate_weight, up_weight, down_weight):
        blk = tokens.shape[0]
        both = jnp.stack([tokens, out_grad])
        both = lax.all_to_all(both, "depth", split_axis=2, concat_axis=1, tiled=True)
        both = lax.all_gather(both, "row", axis=1, tiled=True)
        tok, grad = both[0], both[1]
        partial = jnp.stack(
            [
                jnp.dot(tok, gate_weight, preferred_element_type=jnp.float32),
                jnp.dot(tok, up_weight, preferred_element_type=jnp.float32),
                contract_cols(grad, down_weight),
            ]
        )
        sums = lax.psum_scatter(partial, "depth", scatter_dimension=1, tiled=True)
        terms = jnp.stack(swiglu_terms(sums[0], sums[1], sums[2]))
        hidden, gate_term, up_term = lax.all_gather(terms, "depth", axis=1, tiled=True)
        partial_in = contract_cols(gate_term, gate_weight) + contract_cols(up_term, up_weight)
        width = partial_in.shape[1]
        own = blk // n_col
        partial_in = partial_in.reshape(n_row, n_depth, n_col, own, width)
        partial_in = partial_in.transpose(0, 2, 1, 3, 4).reshape(-1, width)
        input_grad = lax.psum_scatter(
            partial_in, ("row", "col"), scatter_dimension=0, tiled=True
        ).astype(jnp.bfloat16)
        input_grad = lax.all_to_all(
            input_grad, "depth", split_axis=0, concat_axis=1, tiled=True
        )
        return (
            input_grad,
            contract_rows(tok, gate_term).astype(jnp.bfloat16),
            contract_rows(tok, up_term).astype(jnp.bfloat16),
            contract_rows(hidden, grad).astype(jnp.bfloat16),
        )

    return on_device


MESH = pl.DeviceIdType.MESH
CHUNK = 256
BF = jnp.bfloat16


def order_tokens(n_depth, n_row, n_col, own, cuts):
    blk = n_col * own
    rows = n_depth * n_row * blk
    out = np.zeros((cuts * 2 * rows, cuts * 2 * rows), np.float32)
    for cut in range(cuts):
        for a in range(2):
            for r in range(n_row):
                for c in range(n_col):
                    for d in range(n_depth):
                        for t in range(own):
                            to = ((r * n_col + c) * n_depth + d) * own + t
                            at = (((d * n_row + r) * cuts + cut) * 2 + a) * blk + c * own + t
                            out[(cut * 2 + a) * rows + to, at] = 1.0
    return out


def order_owners(n_depth, n_col, own, groups):
    out = np.zeros((n_depth * n_col * 16, groups * n_col * n_depth * own), np.float32)
    for d in range(n_depth):
        for c in range(n_col):
            for g in range(groups):
                for t in range(own):
                    out[(d * n_col + c) * 16 + g * own + t, ((g * n_col + c) * n_depth + d) * own + t] = 1.0
    return out


def chain_kernel(
    n_chunk,
    pk, wg_hbm, wu_hbm, wd_hbm, sel, sel_owner,
    tok_out, grad_out, terms_out, ig_out,
    wg, wu, wd, arrived, tok, grad, keep, core_snd, core_rcv, x_snd, x_rcv, terms, y,
    y_snd, y_rcv, z_snd, z_rcv, f_snd, f_rcv,
    w_sem, a_send, a_recv, a_sem, c_send, c_recv, x_send, x_recv, t_send, t_recv,
    y_send, y_recv, z_send, z_recv, f_send, f_recv, f_sem, o_sem,
):
    d, r, c = lax.axis_index("depth"), lax.axis_index("row"), lax.axis_index("col")
    core, chip = lax.rem(d, 2), lax.div(d, 2)
    mate = d + 1 - 2 * core
    across = d + 2 - 4 * chip
    width = wg.shape[0]
    cw = CHUNK
    half = tok.shape[0] // 2
    zw = width // 4

    def cols_of(j):
        return pl.ds(pl.multiple_of(j * cw, cw), cw)

    def w_copies(j):
        cols = cols_of(j)
        return (
            pltpu.make_async_copy(wg_hbm.at[:, cols], wg.at[:, cols], w_sem.at[0, j]),
            pltpu.make_async_copy(wu_hbm.at[:, cols], wu.at[:, cols], w_sem.at[1, j]),
            pltpu.make_async_copy(wd_hbm.at[cols, :], wd.at[cols, :], w_sem.at[2, j]),
        )

    for j in range(n_chunk):
        for cp in w_copies(j):
            cp.start()

    barrier = pltpu.get_barrier_semaphore()
    me8 = d * 2 + r
    for o in range(1, 8):
        to = lax.rem(me8 + o, 8)
        pl.semaphore_signal(barrier, inc=1, device_id=(lax.div(to, 2), lax.rem(to, 2), c), device_id_type=MESH)
    for oc in range(1, 4):
        for od in range(4):
            pl.semaphore_signal(barrier, inc=1, device_id=(lax.rem(d + od, 4), r, lax.rem(c + oc, 4)), device_id_type=MESH)
    pl.semaphore_wait(barrier, 19)

    blk = pk.shape[1]
    mine = pl.ds(pl.multiple_of(me8 * blk, blk), blk)
    a_copies = []
    for o in range(1, 8):
        to = lax.rem(me8 + o, 8)
        to_d, to_r = lax.div(to, 2), lax.rem(to, 2)
        a_copies.append(pltpu.make_async_remote_copy(
            pk.at[to_d], arrived.at[mine, :], a_send.at[o], a_recv.at[o],
            device_id=(to_d, to_r, c), device_id_type=MESH))
    for cp in a_copies:
        cp.start()
    own_copy = pltpu.make_async_copy(pk.at[d], arrived.at[mine, :], a_sem)
    own_copy.start()
    own_copy.wait()
    y[...] = jnp.zeros_like(y)
    for o in range(1, 8):
        frm = lax.rem(me8 + 8 - o, 8)
        rows = pl.ds(pl.multiple_of(frm * blk, blk), blk)
        pltpu.make_async_remote_copy(
            pk.at[0], arrived.at[rows, :], a_send.at[o], a_recv.at[o],
            device_id=(mate, r, c), device_id_type=MESH).wait_recv()

    n_tok = tok.shape[0]
    part = arrived.shape[1]
    for cut in range(width // part):
        for a, ref in ((0, tok), (1, grad)):
            at = (cut * 2 + a) * n_tok
            ref[:, cut * part:(cut + 1) * part] = jnp.dot(
                sel[at:at + n_tok, :], arrived[...], preferred_element_type=jnp.float32
            ).astype(BF)
    out_copies = [
        pltpu.make_async_copy(tok, tok_out, o_sem.at[0]),
        pltpu.make_async_copy(grad, grad_out, o_sem.at[1]),
    ]
    for cp in out_copies:
        cp.start()

    own_rows = pl.ds(pl.multiple_of(core * half, half), half)
    mate_rows = pl.ds(pl.multiple_of((1 - core) * half, half), half)

    def core_copy(j):
        return pltpu.make_async_remote_copy(
            core_snd.at[j], core_rcv.at[j], c_send.at[j], c_recv.at[j],
            device_id=(mate, r, c), device_id_type=MESH)

    def x_copy(j):
        return pltpu.make_async_remote_copy(
            x_snd.at[j], x_rcv.at[j], x_send.at[j], x_recv.at[j],
            device_id=(across, r, c), device_id_type=MESH)

    def t_copy(j, rows):
        return pltpu.make_async_remote_copy(
            terms.at[:, rows, cols_of(j)], terms.at[:, rows, cols_of(j)],
            t_send.at[j], t_recv.at[j], device_id=(mate, r, c), device_id_type=MESH)

    def forward(j):
        for cp in w_copies(j):
            cp.wait()
        cols = cols_of(j)
        sums = (
            jnp.dot(tok[...], wg[:, cols], preferred_element_type=jnp.float32),
            jnp.dot(tok[...], wu[:, cols], preferred_element_type=jnp.float32),
            contract_cols(grad[...], wd[cols, :]),
        )
        for k, p in enumerate(sums):
            low, high = p[:half], p[half:]
            keep[j, k] = jnp.where(core == 0, low, high)
            core_snd[j, k] = jnp.where(core == 0, high, low).astype(BF)
        core_copy(j).start()

    def chip_sum(j):
        core_copy(j).wait_recv()
        total = keep[j] + core_rcv[j].astype(jnp.float32)
        keep[j] = total
        x_snd[j] = total.astype(BF)
        x_copy(j).start()

    def finish(j):
        x_copy(j).wait_recv()
        total = keep[j] + x_rcv[j].astype(jnp.float32)
        for k, v in enumerate(swiglu_terms(total[0], total[1], total[2])):
            terms[k, own_rows, cols_of(j)] = v
        t_copy(j, own_rows).start()

    def input_sums(j):
        t_copy(j, mate_rows).wait_recv()
        cols = cols_of(j)
        gate_term, up_term = terms[1, :, cols], terms[2, :, cols]
        for n in range(4):
            rows = slice(n * zw, (n + 1) * zw)
            y[:, rows] += contract_cols(gate_term, wg[rows, cols]) + contract_cols(up_term, wu[rows, cols])

    def step(s, _):
        pl.when(s < n_chunk)(lambda: forward(s))
        pl.when((s >= 1) & (s < n_chunk + 1))(lambda: chip_sum(s - 1))
        pl.when((s >= 2) & (s < n_chunk + 2))(lambda: finish(s - 2))
        pl.when(s >= 3)(lambda: input_sums(s - 3))
        return 0

    lax.fori_loop(0, n_chunk + 3, step, 0)
    terms_copy = pltpu.make_async_copy(terms, terms_out, o_sem.at[2])
    terms_copy.start()

    def y_copy(o):
        return pltpu.make_async_remote_copy(
            y_snd.at[o], y_rcv.at[o], y_send.at[o], y_recv.at[o],
            device_id=(d, 1 - r, c), device_id_type=MESH)

    def z_copy(o):
        return pltpu.make_async_remote_copy(
            z_snd.at[o], z_rcv.at[o], z_send.at[o], z_recv.at[o],
            device_id=(d, r, lax.rem(c + o, 4)), device_id_type=MESH)

    row_own = pl.ds(pl.multiple_of(r * half, half), half)
    row_other = pl.ds(pl.multiple_of((1 - r) * half, half), half)

    def z_cols(o):
        return pl.ds(pl.multiple_of(lax.rem(c + o, 4) * zw, zw), zw)

    for o in (2, 1, 3, 0):
        y_snd[o] = y[row_other, z_cols(o)].astype(BF)
        y_copy(o).start()
    for o in (2, 1, 3):
        y_copy(o).wait_recv()
        z_snd[o] = (y[row_own, z_cols(o)] + y_rcv[o].astype(jnp.float32)).astype(BF)
        z_copy(o).start()
    y_copy(0).wait_recv()
    acc = y[row_own, z_cols(0)] + y_rcv[0].astype(jnp.float32)
    for o in (1, 3, 2):
        z_copy(o).wait_recv()
        acc = acc + z_rcv[o].astype(jnp.float32)
    acc = acc.astype(BF)
    stacked = jnp.concatenate([acc[:, g * 128:(g + 1) * 128] for g in range(zw // 128)], axis=0)
    owners = jnp.dot(sel_owner[...], stacked, preferred_element_type=jnp.float32).astype(BF)
    f_snd[...] = owners.reshape(f_snd.shape)

    me16 = d * 4 + c

    def f_copy(o):
        to = lax.rem(me16 + o, 16)
        return pltpu.make_async_remote_copy(
            f_snd.at[to], f_rcv.at[me16], f_send.at[o], f_recv.at[o],
            device_id=(lax.div(to, 4), r, lax.rem(to, 4)), device_id_type=MESH)

    for o in range(1, 16):
        f_copy(o).start()
    f_own = pltpu.make_async_copy(f_snd.at[me16], f_rcv.at[me16], f_sem)
    f_own.start()
    f_own.wait()
    for o in range(1, 16):
        frm = lax.rem(me16 + 16 - o, 16)
        pltpu.make_async_remote_copy(
            f_snd.at[0], f_rcv.at[frm], f_send.at[o], f_recv.at[o],
            device_id=(mate, r, c), device_id_type=MESH).wait_recv()
    ig_out[...] = f_rcv[...]

    for cp in a_copies:
        cp.wait_send()

    def drain(j, _):
        core_copy(j).wait_send()
        x_copy(j).wait_send()
        t_copy(j, own_rows).wait_send()
        return 0

    lax.fori_loop(0, n_chunk, drain, 0)
    for o in range(4):
        y_copy(o).wait_send()
    for o in range(1, 4):
        z_copy(o).wait_send()
    for o in range(1, 16):
        f_copy(o).wait_send()
    for cp in out_copies:
        cp.wait()
    terms_copy.wait()


def fused(n_depth, n_row, n_col):
    def on_device(tokens, out_grad, gate_weight, up_weight, down_weight):
        blk, model = tokens.shape
        width, units = gate_weight.shape
        own = blk // n_col
        n_tok = n_depth * n_row * blk
        cuts, part = 2, width // 2
        n_chunk = units // CHUNK
        half = n_tok // 2
        zw = width // n_col
        groups = zw // 128
        pk = jnp.stack([tokens, out_grad]).reshape(2, blk, n_depth, cuts, part)
        pk = pk.transpose(2, 3, 0, 1, 4).reshape(n_depth, cuts * 2 * blk, part)
        sel = jnp.asarray(order_tokens(n_depth, n_row, n_col, own, cuts), BF)
        sel_owner = jnp.asarray(order_owners(n_depth, n_col, own, groups), BF)
        sel_owner = sel_owner.reshape(n_depth * n_col * 16, -1)
        vmem, hbm = pl.BlockSpec(memory_space=pltpu.VMEM), pl.BlockSpec(memory_space=pl.ANY)
        dma = pltpu.SemaphoreType.DMA
        tok, grad, terms, ig = pl.pallas_call(
            functools.partial(chain_kernel, n_chunk),
            out_shape=(
                jax.ShapeDtypeStruct((n_tok, width), BF),
                jax.ShapeDtypeStruct((n_tok, width), BF),
                jax.ShapeDtypeStruct((3, n_tok, units), BF),
                jax.ShapeDtypeStruct((16, 16, 128), BF),
            ),
            in_specs=[vmem, hbm, hbm, hbm, vmem, vmem],
            out_specs=(hbm, hbm, hbm, vmem),
            scratch_shapes=[
                pltpu.VMEM((width, units), BF),
                pltpu.VMEM((width, units), BF),
                pltpu.VMEM((units, width), BF),
                pltpu.VMEM((n_depth * n_row * cuts * 2 * blk, part), BF),
                pltpu.VMEM((n_tok, width), BF),
                pltpu.VMEM((n_tok, width), BF),
                pltpu.VMEM((n_chunk, 3, half, CHUNK), jnp.float32),
                pltpu.VMEM((n_chunk, 3, half, CHUNK), BF),
                pltpu.VMEM((n_chunk, 3, half, CHUNK), BF),
                pltpu.VMEM((n_chunk, 3, half, CHUNK), BF),
                pltpu.VMEM((n_chunk, 3, half, CHUNK), BF),
                pltpu.VMEM((3, n_tok, units), BF),
                pltpu.VMEM((n_tok, width), jnp.float32),
                pltpu.VMEM((4, half, zw), BF),
                pltpu.VMEM((4, half, zw), BF),
                pltpu.VMEM((4, half, zw), BF),
                pltpu.VMEM((4, half, zw), BF),
                pltpu.VMEM((16, 16, 128), BF),
                pltpu.VMEM((16, 16, 128), BF),
                dma((3, n_chunk)),
                dma((8,)), dma((8,)), dma,
                dma((n_chunk,)), dma((n_chunk,)),
                dma((n_chunk,)), dma((n_chunk,)),
                dma((n_chunk,)), dma((n_chunk,)),
                dma((4,)), dma((4,)),
                dma((4,)), dma((4,)),
                dma((16,)), dma((16,)), dma,
                dma((3,)),
            ],
            compiler_params=pltpu.CompilerParams(
                collective_id=0, has_side_effects=True, vmem_limit_bytes=56 * 1024 * 1024
            ),
            cost_estimate=pl.CostEstimate(
                flops=10 * n_tok * width * units, bytes_accessed=6 * width * units, transcendentals=n_tok * units
            ),
        )(pk, gate_weight, up_weight, down_weight, sel, sel_owner)
        ig = ig.reshape(n_depth, n_col, 16, 128)[:, :, :groups * own]
        ig = ig.reshape(n_depth, n_col, groups, own, 128).transpose(3, 0, 1, 2, 4)
        return (
            ig.reshape(own, model),
            contract_rows(tok, terms[1]).astype(BF),
            contract_rows(tok, terms[2]).astype(BF),
            contract_rows(terms[0], grad).astype(BF),
        )

    return on_device


def solution(mesh):
    sizes = mesh.shape
    shape = (sizes["depth"], sizes["row"], sizes["col"])
    on_device = fused(*shape) if shape == (4, 2, 4) else weight_stationary(*shape)
    return jax.shard_map(
        on_device,
        mesh=mesh,
        in_specs=(
            P(("depth", "row"), None),
            P(("depth", "row"), None),
            P("depth", ("row", "col")),
            P("depth", ("row", "col")),
            P(("row", "col"), "depth"),
        ),
        out_specs=(
            P(("depth", "row", "col"), None),
            P("depth", ("row", "col")),
            P("depth", ("row", "col")),
            P(("row", "col"), "depth"),
        ),
        check_vma=False,
    )
```

time: 1370 us -> 82.5 us (0.06)
  waiting for transfers between devices: 1120 us -> 0 us
  matrix products: 132 us -> 18.4 us
  blocking collectives: 67.9 us -> 0 us
  Pallas kernels: 0 us -> 57.9 us
  local copies, waits for them, and re-layouts: 26.3 us -> 4.87 us
  between operations: 14.8 us -> 0.7 us
    reduce_scatter x3 -> x0, waiting for transfers between devices: 562 us -> none  [the longest x1 225 us: on_device(): lax.psum_scatter(contract_rows(hidden, all_grad).astype(jnp.bfloat16), 'd...]
    all_gather x3 -> x0, waiting for transfers between devices: 560 us -> none  [the longest x1 187 us: on_device(): lax.all_gather(down_weight, 'depth', axis=1, tiled=True)]
    dot_general x5 -> x0, matrix products: 76.9 us -> none  [the longest x3 45.1 us: contract_cols(): lax.dot_general(left, right, (((1,), (1,)), ((), ())), preferred_element_...]
    pallas_call x0 -> x1, Pallas kernels: none -> 57.9 us  [on_device(): pl.pallas_call(functools.partial(chain_kernel, n_chunk), out_shape=(jax.S...]
    unnamed x1 -> x0, blocking collectives: 49.3 us -> none
    dot_general x3, matrix products: 55.5 us -> 18.4 us  [contract_rows(): lax.dot_general(left, right, (((0,), (0,)), ((), ())), preferred_element_...]
    unnamed x7 -> x5, local copies, waits for them, and re-layouts: 25.6 us -> 0.98 us
    all_gather x2 -> x0, blocking collectives: 18.6 us -> none  [the longest x1 10.2 us: on_device(): lax.all_gather(tokens, 'row', axis=0, tiled=True)]
  transfers between devices with their start and end apart: 6 -> 0, of which waited for: 6 -> 0; matrix products, arithmetic and copies ran while one was open for 10% -> 0% of each run, Pallas kernels for 0% -> 0%
where the time goes in v1:
time: 82.5 us; the launch traced here: 82.2 us
  Pallas kernels  57.9 us (70%)
  matrix products  18.4 us (22%)
  local copies, waits for them, and re-layouts  4.87 us (6%)
    pallas_call x1, Pallas kernels, on_device(): pl.pallas_call(functools.partial(chain_kernel, n_chunk), out_shape=(jax.S...  57.9 us
    dot_general x3, matrix products, contract_rows(): lax.dot_general(left, right, (((0,), (0,)), ((), ())), preferred_element_...  18.4 us
    another operation x4, local copies, waits for them, and re-layouts, on_device(): pk = jnp.stack([tokens, out_grad]).reshape(2, blk, n_depth, cuts, part)  2.34 us

profile of v1, /device:TPU:0, one launch (start us, length us, event | category | flops | bytes accessed | tf_op | source)
XLA Modules:
  0.0 82.2 jit_solution(12242042519014675739)
XLA Ops:
  0.6 1.1 %stack.9 = bf16[1,12,4,2,1024]{4,3,2,1,0:T(2,128)(2,1)S(1)} reshape(bf16[12,8192]{1,0:T(8,128)(2,1)} %param.7) | data formatting | bytes 393216 | tf_op jit(solution)/shard_map/stack | solution.py:333
  1.7 0.1 copy.18
  1.8 1.1 %stack.10 = bf16[1,12,4,2,1024]{4,3,2,1,0:T(2,128)(2,1)S(1)} reshape(bf16[12,8192]{1,0:T(8,128)(2,1)} %param.8) | data formatting | bytes 393216 | tf_op jit(solution)/shard_map/stack | solution.py:333
  2.9 0.1 copy.19
  3.0 0.3 pad_maximum_fusion
  3.3 0.9 %copy.20.pk = bf16[4,48,1024]{2,1,0:T(8,128)(2,1)} copy(bf16[4,48,1024]{2,0,1:T(4,128)(2,1)S(1)} %bitcast.20) | data formatting | bytes 786432 | tf_op jit(solution)/shard_map/reshape | solution.py:334
  4.1 57.9 %shard_map.102 = (bf16[96,2048]{1,0:T(8,128)(2,1)}, bf16[96,2048]{1,0:T(8,128)(2,1)}, bf16[3,96,2048]{2,1,0:T(8,128)(2,1)}, bf16[16,16,128]{2,1,0:T(8,128)(2,1)}) custom-call(bf16[4,48,1024]{2,1,0:T(8,128)(2,1)} %copy.20.pk, bf16[2048,2048]{1,0:T(8,128)(2,1)} %wg_hbm.1, bf16[2048,2048]{1,0:T(8,128)(2,1)} %wu_hbm.1, bf16[2048,2048]{1,0:T(8,128)(2,1)} %wd_hbm.1, ...), custom_call_target="tpu_custom_call" | custom-call | flops 4026531840 | bytes 25165824 | tf_op jit(solution)/shard_map/pallas_call | solution.py:340
  62.1 0.0 copy-start
  62.1 0.0 copy-start.1
  62.1 1.0 %copy.23 = bf16[4,4,12,128]{3,1,2,0:T(4,128)(2,1)S(1)} copy(bf16[4,4,12,128]{3,2,1,0:T(8,128)(2,1)} %bitcast.22) | data formatting | bytes 98304
  63.1 0.7 reshape.28
  63.8 6.9 %convolution_convert_fusion = bf16[2048,2048]{1,0:T(8,128)(2,1)} fusion(bf16[96,2048]{1,0:T(8,128)(2,1)} %get-tuple-element.11, bf16[3,96,2048]{2,1,0:T(8,128)(2,1)} %get-tuple-element.10), kind=kOutput, calls=%fused_computation | convolution fusion | flops 809500672 | bytes 9175040 | tf_op jit(solution)/shard_map/dot_general | solution.py:13
  70.7 0.0 copy-done
  70.7 0.0 copy-done.1
  70.7 5.8 %convolution_convert_fusion.1 = bf16[2048,2048]{1,0:T(8,128)(2,1)} fusion(bf16[96,2048]{1,0:T(8,128)(2,1)S(1)} %copy-done, bf16[3,96,2048]{2,1,0:T(8,128)(2,1)S(1)} %copy-done.1), kind=kOutput, calls=%fused_computation.1 | convolution fusion | flops 809500672 | bytes 9175040 | tf_op jit(solution)/shard_map/dot_general | solution.py:13
  76.4 5.8 %convolution_convert_fusion.2 = bf16[2048,2048]{1,0:T(8,128)(2,1)} fusion(bf16[96,2048]{1,0:T(8,128)(2,1)S(1)} %copy-done, bf16[3,96,2048]{2,1,0:T(8,128)(2,1)S(1)} %copy-done.1), kind=kOutput, calls=%fused_computation.2 | convolution fusion | flops 809500672 | bytes 9175040 | tf_op jit(solution)/shard_map/dot_general | solution.py:13
  (1 shorter events, 0.0 us)
Async XLA Ops:
  62.1 8.6 %copy-start = (bf16[96,2048]{1,0:T(8,128)(2,1)S(1)}, bf16[96,2048]{1,0:T(8,128)(2,1)}, u32[]{:S(2)}) copy-start(bf16[96,2048]{1,0:T(8,128)(2,1)} %get-tuple-element.9) | copy-start | bytes 1179652
  62.1 8.6 %copy-start.1 = (bf16[3,96,2048]{2,1,0:T(8,128)(2,1)S(1)}, bf16[3,96,2048]{2,1,0:T(8,128)(2,1)}, u32[]{:S(2)}) copy-start(bf16[3,96,2048]{2,1,0:T(8,128)(2,1)} %get-tuple-element.10) | copy-start | bytes 3538948

commit v2 on v1

--- a/solution.py
+++ b/solution.py
@@ -76,16 +76,14 @@
 def order_tokens(n_depth, n_row, n_col, own, cuts):
     blk = n_col * own
     rows = n_depth * n_row * blk
-    out = np.zeros((cuts * 2 * rows, cuts * 2 * rows), np.float32)
+    out = np.zeros((cuts * rows, cuts * rows), np.float32)
     for cut in range(cuts):
-        for a in range(2):
-            for r in range(n_row):
-                for c in range(n_col):
-                    for d in range(n_depth):
-                        for t in range(own):
-                            to = ((r * n_col + c) * n_depth + d) * own + t
-                            at = (((d * n_row + r) * cuts + cut) * 2 + a) * blk + c * own + t
-                            out[(cut * 2 + a) * rows + to, at] = 1.0
+        for r in range(n_row):
+            for c in range(n_col):
+                for d in range(n_depth):
+                    for t in range(own):
+                        to = ((r * n_col + c) * n_depth + d) * own + t
+                        out[cut * rows + to, ((d * n_row + r) * cuts + cut) * blk + c * own + t] = 1.0
     return out
 
 
@@ -101,9 +99,9 @@
 
 def chain_kernel(
     n_chunk,
-    pk, wg_hbm, wu_hbm, wd_hbm, sel, sel_owner,
+    tok_in, grad_in, wg_hbm, wu_hbm, wd_hbm, sel, sel_owner,
     tok_out, grad_out, terms_out, ig_out,
-    wg, wu, wd, arrived, tok, grad, keep, core_snd, core_rcv, x_snd, x_rcv, terms, y,
+    pk, stage, wg, wu, wd, arrived, tok, grad, keep, core_snd, core_rcv, x_snd, x_rcv, terms, y,
     y_snd, y_rcv, z_snd, z_rcv, f_snd, f_rcv,
     w_sem, a_send, a_recv, a_sem, c_send, c_recv, x_send, x_recv, t_send, t_recv,
     y_send, y_recv, z_send, z_recv, f_send, f_recv, f_sem, o_sem,
@@ -120,17 +118,16 @@
     def cols_of(j):
         return pl.ds(pl.multiple_of(j * cw, cw), cw)
 
-    def w_copies(j):
+    def w_copy(j, k):
         cols = cols_of(j)
-        return (
-            pltpu.make_async_copy(wg_hbm.at[:, cols], wg.at[:, cols], w_sem.at[0, j]),
-            pltpu.make_async_copy(wu_hbm.at[:, cols], wu.at[:, cols], w_sem.at[1, j]),
-            pltpu.make_async_copy(wd_hbm.at[cols, :], wd.at[cols, :], w_sem.at[2, j]),
-        )
-
-    for j in range(n_chunk):
-        for cp in w_copies(j):
-            cp.start()
+        at = (cols, slice(None)) if k == 2 else (slice(None), cols)
+        src, dst = ((wg_hbm, wg), (wu_hbm, wu), (wd_hbm, wd))[k]
+        return pltpu.make_async_copy(src.at[at], dst.at[at], w_sem.at[k, j])
+
+    for k in ((0, 1), (2,)):
+        for j in range(n_chunk):
+            for i in k:
+                w_copy(j, i).start()
 
     barrier = pltpu.get_barrier_semaphore()
     me8 = d * 2 + r
@@ -140,56 +137,63 @@
     for oc in range(1, 4):
         for od in range(4):
             pl.semaphore_signal(barrier, inc=1, device_id=(lax.rem(d + od, 4), r, lax.rem(c + oc, 4)), device_id_type=MESH)
+    blk, part = pk.shape[2:]
+    cuts = width // part
+    own_blk = blk // cuts
+    for a, ref in ((0, tok_in), (1, grad_in)):
+        for q in range(4):
+            for h in range(cuts):
+                at = q * width + h * part
+                stage[h * own_blk:(h + 1) * own_blk, :] = ref[:, at:at + part].astype(jnp.float32)
+            pk[a, q] = stage[...].astype(BF)
+    y[...] = jnp.zeros_like(y)
     pl.semaphore_wait(barrier, 19)
 
-    blk = pk.shape[1]
     mine = pl.ds(pl.multiple_of(me8 * blk, blk), blk)
     a_copies = []
-    for o in range(1, 8):
-        to = lax.rem(me8 + o, 8)
-        to_d, to_r = lax.div(to, 2), lax.rem(to, 2)
-        a_copies.append(pltpu.make_async_remote_copy(
-            pk.at[to_d], arrived.at[mine, :], a_send.at[o], a_recv.at[o],
-            device_id=(to_d, to_r, c), device_id_type=MESH))
+    for a in range(2):
+        for o in range(1, 8):
+            to = lax.rem(me8 + o, 8)
+            to_d, to_r = lax.div(to, 2), lax.rem(to, 2)
+            a_copies.append(pltpu.make_async_remote_copy(
+                pk.at[a, to_d], arrived.at[a, mine, :], a_send.at[a, o], a_recv.at[a, o],
+                device_id=(to_d, to_r, c), device_id_type=MESH))
     for cp in a_copies:
         cp.start()
-    own_copy = pltpu.make_async_copy(pk.at[d], arrived.at[mine, :], a_sem)
-    own_copy.start()
-    own_copy.wait()
-    y[...] = jnp.zeros_like(y)
-    for o in range(1, 8):
-        frm = lax.rem(me8 + 8 - o, 8)
-        rows = pl.ds(pl.multiple_of(frm * blk, blk), blk)
-        pltpu.make_async_remote_copy(
-            pk.at[0], arrived.at[rows, :], a_send.at[o], a_recv.at[o],
-            device_id=(mate, r, c), device_id_type=MESH).wait_recv()
-
+    own_copies = [pltpu.make_async_copy(pk.at[a, d], arrived.at[a, mine, :], a_sem.at[a]) for a in range(2)]
+    for cp in own_copies:
+        cp.start()
     n_tok = tok.shape[0]
-    part = arrived.shape[1]
-    for cut in range(width // part):
-        for a, ref in ((0, tok), (1, grad)):
-            at = (cut * 2 + a) * n_tok
-            ref[:, cut * part:(cut + 1) * part] = jnp.dot(
-                sel[at:at + n_tok, :], arrived[...], preferred_element_type=jnp.float32
+
+    def take(a, ref, out):
+        own_copies[a].wait()
+        for o in range(1, 8):
+            frm = lax.rem(me8 + 8 - o, 8)
+            rows = pl.ds(pl.multiple_of(frm * blk, blk), blk)
+            pltpu.make_async_remote_copy(
+                pk.at[a, 0], arrived.at[a, rows, :], a_send.at[a, o], a_recv.at[a, o],
+                device_id=(mate, r, c), device_id_type=MESH).wait_recv()
+        for h in range(cuts):
+            ref[:, h * part:(h + 1) * part] = jnp.dot(
+                sel[h * n_tok:(h + 1) * n_tok, :], arrived[a], preferred_element_type=jnp.float32
             ).astype(BF)
-    out_copies = [
-        pltpu.make_async_copy(tok, tok_out, o_sem.at[0]),
-        pltpu.make_async_copy(grad, grad_out, o_sem.at[1]),
-    ]
-    for cp in out_copies:
+        cp = pltpu.make_async_copy(ref, out, o_sem.at[a])
         cp.start()
+        return cp
 
     own_rows = pl.ds(pl.multiple_of(core * half, half), half)
     mate_rows = pl.ds(pl.multiple_of((1 - core) * half, half), half)
 
-    def core_copy(j):
-        return pltpu.make_async_remote_copy(
-            core_snd.at[j], core_rcv.at[j], c_send.at[j], c_recv.at[j],
+    def core_copy(j, g):
+        ks = pl.ds(0, 2) if g == 0 else pl.ds(2, 1)
+        return pltpu.make_async_remote_copy(
+            core_snd.at[j, ks], core_rcv.at[j, ks], c_send.at[g, j], c_recv.at[g, j],
             device_id=(mate, r, c), device_id_type=MESH)
 
-    def x_copy(j):
-        return pltpu.make_async_remote_copy(
-            x_snd.at[j], x_rcv.at[j], x_send.at[j], x_recv.at[j],
+    def x_copy(j, g):
+        ks = pl.ds(0, 2) if g == 0 else pl.ds(2, 1)
+        return pltpu.make_async_remote_copy(
+            x_snd.at[j, ks], x_rcv.at[j, ks], x_send.at[g, j], x_recv.at[g, j],
             device_id=(across, r, c), device_id_type=MESH)
 
     def t_copy(j, rows):
@@ -197,30 +201,34 @@
             terms.at[:, rows, cols_of(j)], terms.at[:, rows, cols_of(j)],
             t_send.at[j], t_recv.at[j], device_id=(mate, r, c), device_id_type=MESH)
 
-    def forward(j):
-        for cp in w_copies(j):
-            cp.wait()
+    def split(j, k, p):
+        low, high = p[:half], p[half:]
+        keep[j, k] = jnp.where(core == 0, low, high)
+        core_snd[j, k] = jnp.where(core == 0, high, low).astype(BF)
+
+    def forward(j, g):
         cols = cols_of(j)
-        sums = (
-            jnp.dot(tok[...], wg[:, cols], preferred_element_type=jnp.float32),
-            jnp.dot(tok[...], wu[:, cols], preferred_element_type=jnp.float32),
-            contract_cols(grad[...], wd[cols, :]),
-        )
-        for k, p in enumerate(sums):
-            low, high = p[:half], p[half:]
-            keep[j, k] = jnp.where(core == 0, low, high)
-            core_snd[j, k] = jnp.where(core == 0, high, low).astype(BF)
-        core_copy(j).start()
-
-    def chip_sum(j):
-        core_copy(j).wait_recv()
-        total = keep[j] + core_rcv[j].astype(jnp.float32)
-        keep[j] = total
-        x_snd[j] = total.astype(BF)
-        x_copy(j).start()
+        if g == 0:
+            w_copy(j, 0).wait()
+            w_copy(j, 1).wait()
+            split(j, 0, jnp.dot(tok[...], wg[:, cols], preferred_element_type=jnp.float32))
+            split(j, 1, jnp.dot(tok[...], wu[:, cols], preferred_element_type=jnp.float32))
+        else:
+            w_copy(j, 2).wait()
+            split(j, 2, contract_cols(grad[...], wd[cols, :]))
+        core_copy(j, g).start()
+
+    def chip_sum(j, g):
+        core_copy(j, g).wait_recv()
+        for k in ((0, 1), (2,))[g]:
+            total = keep[j, k] + core_rcv[j, k].astype(jnp.float32)
+            keep[j, k] = total
+            x_snd[j, k] = total.astype(BF)
+        x_copy(j, g).start()
 
     def finish(j):
-        x_copy(j).wait_recv()
+        x_copy(j, 0).wait_recv()
+        x_copy(j, 1).wait_recv()
         total = keep[j] + x_rcv[j].astype(jnp.float32)
         for k, v in enumerate(swiglu_terms(total[0], total[1], total[2])):
             terms[k, own_rows, cols_of(j)] = v
@@ -234,13 +242,22 @@
             rows = slice(n * zw, (n + 1) * zw)
             y[:, rows] += contract_cols(gate_term, wg[rows, cols]) + contract_cols(up_term, wu[rows, cols])
 
+    def tok_step(s, _):
+        forward(s, 0)
+        pl.when(s >= 1)(lambda: chip_sum(s - 1, 0))
+        return 0
+
     def step(s, _):
-        pl.when(s < n_chunk)(lambda: forward(s))
-        pl.when((s >= 1) & (s < n_chunk + 1))(lambda: chip_sum(s - 1))
+        pl.when(s < n_chunk)(lambda: forward(s, 1))
+        pl.when((s >= 1) & (s < n_chunk + 1))(lambda: chip_sum(s - 1, 1))
         pl.when((s >= 2) & (s < n_chunk + 2))(lambda: finish(s - 2))
         pl.when(s >= 3)(lambda: input_sums(s - 3))
         return 0
 
+    out_copies = [take(0, tok, tok_out)]
+    lax.fori_loop(0, n_chunk, tok_step, 0)
+    chip_sum(n_chunk - 1, 0)
+    out_copies.append(take(1, grad, grad_out))
     lax.fori_loop(0, n_chunk + 3, step, 0)
     terms_copy = pltpu.make_async_copy(terms, terms_out, o_sem.at[2])
     terms_copy.start()
@@ -302,8 +319,9 @@
         cp.wait_send()
 
     def drain(j, _):
-        core_copy(j).wait_send()
-        x_copy(j).wait_send()
+        for g in range(2):
+            core_copy(j, g).wait_send()
+            x_copy(j, g).wait_send()
         t_copy(j, own_rows).wait_send()
         return 0
 
@@ -319,19 +337,32 @@
     terms_copy.wait()
 
 
+def grads_kernel(own, groups, tok, grad, hidden, gate_term, up_term, ig, ig_out, gate_grad, up_grad, down_grad, wide, line):
+    def assemble():
+        wide[...] = ig[...].astype(jnp.float32)
+        for n in range(ig.shape[0]):
+            for g in range(groups):
+                at = (n * groups + g) * 128
+                line[0:own, at:at + 128] = wide[n, g * own:(g + 1) * own, :]
+        ig_out[...] = line[0:own, :].astype(BF)
+
+    pl.when(pl.program_id(0) == 0)(assemble)
+    gate_grad[...] = contract_rows(tok[...], gate_term[0]).astype(BF)
+    up_grad[...] = contract_rows(tok[...], up_term[0]).astype(BF)
+    down_grad[...] = contract_rows(hidden[0], grad[...]).astype(BF)
+
+
 def fused(n_depth, n_row, n_col):
     def on_device(tokens, out_grad, gate_weight, up_weight, down_weight):
         blk, model = tokens.shape
         width, units = gate_weight.shape
         own = blk // n_col
         n_tok = n_depth * n_row * blk
-        cuts, part = 2, width // 2
+        cuts, part = 4, width // 4
         n_chunk = units // CHUNK
         half = n_tok // 2
         zw = width // n_col
         groups = zw // 128
-        pk = jnp.stack([tokens, out_grad]).reshape(2, blk, n_depth, cuts, part)
-        pk = pk.transpose(2, 3, 0, 1, 4).reshape(n_depth, cuts * 2 * blk, part)
         sel = jnp.asarray(order_tokens(n_depth, n_row, n_col, own, cuts), BF)
         sel_owner = jnp.asarray(order_owners(n_depth, n_col, own, groups), BF)
         sel_owner = sel_owner.reshape(n_depth * n_col * 16, -1)
@@ -345,13 +376,15 @@
                 jax.ShapeDtypeStruct((3, n_tok, units), BF),
                 jax.ShapeDtypeStruct((16, 16, 128), BF),
             ),
-            in_specs=[vmem, hbm, hbm, hbm, vmem, vmem],
+            in_specs=[vmem, vmem, hbm, hbm, hbm, vmem, vmem],
             out_specs=(hbm, hbm, hbm, vmem),
             scratch_shapes=[
+                pltpu.VMEM((2, n_depth, cuts * blk, part), BF),
+                pltpu.VMEM((cuts * blk, part), jnp.float32),
                 pltpu.VMEM((width, units), BF),
                 pltpu.VMEM((width, units), BF),
                 pltpu.VMEM((units, width), BF),
-                pltpu.VMEM((n_depth * n_row * cuts * 2 * blk, part), BF),
+                pltpu.VMEM((2, n_depth * n_row * cuts * blk, part), BF),
                 pltpu.VMEM((n_tok, width), BF),
                 pltpu.VMEM((n_tok, width), BF),
                 pltpu.VMEM((n_chunk, 3, half, CHUNK), jnp.float32),
@@ -368,9 +401,9 @@
                 pltpu.VMEM((16, 16, 128), BF),
                 pltpu.VMEM((16, 16, 128), BF),
                 dma((3, n_chunk)),
-                dma((8,)), dma((8,)), dma,
-                dma((n_chunk,)), dma((n_chunk,)),
-                dma((n_chunk,)), dma((n_chunk,)),
+                dma((2, 8)), dma((2, 8)), dma((2,)),
+                dma((2, n_chunk)), dma((2, n_chunk)),
+                dma((2, n_chunk)), dma((2, n_chunk)),
                 dma((n_chunk,)), dma((n_chunk,)),
                 dma((4,)), dma((4,)),
                 dma((4,)), dma((4,)),
@@ -383,15 +416,31 @@
             cost_estimate=pl.CostEstimate(
                 flops=10 * n_tok * width * units, bytes_accessed=6 * width * units, transcendentals=n_tok * units
             ),
-        )(pk, gate_weight, up_weight, down_weight, sel, sel_owner)
-        ig = ig.reshape(n_depth, n_col, 16, 128)[:, :, :groups * own]
-        ig = ig.reshape(n_depth, n_col, groups, own, 128).transpose(3, 0, 1, 2, 4)
-        return (
-            ig.reshape(own, model),
-            contract_rows(tok, terms[1]).astype(BF),
-            contract_rows(tok, terms[2]).astype(BF),
-            contract_rows(terms[0], grad).astype(BF),
-        )
+        )(tokens, out_grad, gate_weight, up_weight, down_weight, sel, sel_owner)
+        rows = 256
+        full = lambda *shape: pl.BlockSpec(shape, lambda i: (0,) * len(shape))
+        by_rows = pl.BlockSpec((rows, width), lambda i: (i, 0))
+        return pl.pallas_call(
+            functools.partial(grads_kernel, own, groups),
+            grid=(width // rows,),
+            out_shape=(
+                jax.ShapeDtypeStruct((own, model), BF),
+                jax.ShapeDtypeStruct((width, units), BF),
+                jax.ShapeDtypeStruct((width, units), BF),
+                jax.ShapeDtypeStruct((units, width), BF),
+            ),
+            in_specs=[
+                pl.BlockSpec((n_tok, rows), lambda i: (0, i)),
+                full(n_tok, width),
+                pl.BlockSpec((1, n_tok, rows), lambda i: (0, 0, i)),
+                pl.BlockSpec((1, n_tok, units), lambda i: (1, 0, 0)),
+                pl.BlockSpec((1, n_tok, units), lambda i: (2, 0, 0)),
+                full(16, 16, 128),
+            ],
+            out_specs=(full(own, model), by_rows, by_rows, by_rows),
+            scratch_shapes=[pltpu.VMEM((16, 16, 128), jnp.float32), pltpu.VMEM((8, model), jnp.float32)],
+            compiler_params=pltpu.CompilerParams(vmem_limit_bytes=48 * 1024 * 1024),
+        )(tok, grad, terms, terms, terms, ig)
 
     return on_device
 

time: 82.5 us -> 73.6 us (0.89)
  matrix products: 18.4 us -> 0 us
  Pallas kernels: 57.9 us -> 68.5 us
    dot_general x3 -> x0, matrix products: 18.4 us -> none  [contract_rows(): lax.dot_general(left, right, (((0,), (0,)), ((), ())), preferred_element_...]
    pallas_call x0 -> x1, Pallas kernels: none -> 10.6 us  [on_device(): pl.pallas_call(functools.partial(grads_kernel, own, groups), grid=(width...]
    unnamed x5 -> x8, local copies, waits for them, and re-layouts: 0.98 us -> 4.09 us
    another operation x4 -> x0, local copies, waits for them, and re-layouts: 2.34 us -> none  [on_device(): pk = jnp.stack([tokens, out_grad]).reshape(2, blk, n_depth, cuts, part)]
    reshape x2 -> x0, local copies, waits for them, and re-layouts: 1.52 us -> none  [the longest x1 0.87 us: on_device(): pk = pk.transpose(2, 3, 0, 1, 4).reshape(n_depth, cuts * 2 * blk, part)]
where the time goes in v2:
time: 73.6 us; the launch traced here: 73.3 us
  Pallas kernels  68.5 us (93%)
  local copies, waits for them, and re-layouts  4.09 us (6%)
    pallas_call x1, Pallas kernels, on_device(): pl.pallas_call(functools.partial(chain_kernel, n_chunk), out_shape=(jax.S...  57.9 us
    pallas_call x1, Pallas kernels, on_device(): pl.pallas_call(functools.partial(grads_kernel, own, groups), grid=(width...  10.6 us
    unnamed x8, local copies, waits for them, and re-layouts  4.09 us

profile of v2, /device:TPU:0, one launch (start us, length us, event | category | flops | bytes accessed | tf_op | source)
XLA Modules:
  0.0 73.3 jit_solution(4976366082404992551)
XLA Ops:
  0.6 57.9 %shard_map.102 = (bf16[96,2048]{1,0:T(8,128)(2,1)}, bf16[96,2048]{1,0:T(8,128)(2,1)}, bf16[3,96,2048]{2,1,0:T(8,128)(2,1)}, bf16[16,16,128]{2,1,0:T(8,128)(2,1)}) custom-call(bf16[12,8192]{1,0:T(8,128)(2,1)} %tok_in.1, bf16[12,8192]{1,0:T(8,128)(2,1)} %grad_in.1, bf16[2048,2048]{1,0:T(8,128)(2,1)} %wg_hbm.1, bf16[2048,2048]{1,0:T(8,128)(2,1)} %wu_hbm.1, ...), custom_call_target="tpu_custom_call" | custom-call | flops 4026531840 | bytes 25165824 | tf_op jit(solution)/shard_map/pallas_call | solution.py:371
  58.6 0.0 copy-start
  58.6 1.3 %copy-done = bf16[3,96,2048]{2,1,0:T(8,128)(2,1)S(1)} copy-done((bf16[3,96,2048]{2,1,0:T(8,128)(2,1)S(1)}, bf16[3,96,2048]{2,1,0:T(8,128)(2,1)}, u32[]{:S(2)}) %copy-start) | copy-done | bytes 1179672
  59.9 0.0 copy-start.1
  59.9 1.0 %copy-done.1 = bf16[96,2048]{1,0:T(8,128)(2,1)S(1)} copy-done((bf16[96,2048]{1,0:T(8,128)(2,1)S(1)}, bf16[96,2048]{1,0:T(8,128)(2,1)}, u32[]{:S(2)}) %copy-start.1) | copy-done | bytes 393240
  60.9 0.0 copy-start.2
  60.9 1.0 %copy-done.2 = bf16[96,2048]{1,0:T(8,128)(2,1)S(1)} copy-done((bf16[96,2048]{1,0:T(8,128)(2,1)S(1)}, bf16[96,2048]{1,0:T(8,128)(2,1)}, u32[]{:S(2)}) %copy-start.2) | copy-done | bytes 393240
  61.9 0.0 copy-start.3
  61.9 0.8 %copy-done.3 = bf16[16,16,128]{2,1,0:T(8,128)(2,1)S(1)} copy-done((bf16[16,16,128]{2,1,0:T(8,128)(2,1)S(1)}, bf16[16,16,128]{2,1,0:T(8,128)(2,1)}, u32[]{:S(2)}) %copy-start.3) | copy-done | bytes 65560
  62.7 10.6 %shard_map.103 = (bf16[3,8192]{1,0:T(4,128)(2,1)}, bf16[2048,2048]{1,0:T(8,128)(2,1)}, bf16[2048,2048]{1,0:T(8,128)(2,1)}, bf16[2048,2048]{1,0:T(8,128)(2,1)}) custom-call(bf16[96,2048]{1,0:T(8,128)(2,1)S(1)} %copy-done.1, bf16[96,2048]{1,0:T(8,128)(2,1)S(1)} %copy-done.2, bf16[3,96,2048]{2,1,0:T(8,128)(2,1)S(1)} %copy-done, ...), custom_call_target="tpu_custom_call" | custom-call | tf_op jit(solution)/shard_map/pallas_call | solution.py:423
Async XLA Ops:
  58.6 1.3 %copy-start = (bf16[3,96,2048]{2,1,0:T(8,128)(2,1)S(1)}, bf16[3,96,2048]{2,1,0:T(8,128)(2,1)}, u32[]{:S(2)}) copy-start(bf16[3,96,2048]{2,1,0:T(8,128)(2,1)} %get-tuple-element.10.hidden.gate_term.up_term) | copy-start | bytes 3538948
  59.9 1.0 %copy-start.1 = (bf16[96,2048]{1,0:T(8,128)(2,1)S(1)}, bf16[96,2048]{1,0:T(8,128)(2,1)}, u32[]{:S(2)}) copy-start(bf16[96,2048]{1,0:T(8,128)(2,1)} %get-tuple-element.8.tok) | copy-start | bytes 1179652
  60.9 1.0 %copy-start.2 = (bf16[96,2048]{1,0:T(8,128)(2,1)S(1)}, bf16[96,2048]{1,0:T(8,128)(2,1)}, u32[]{:S(2)}) copy-start(bf16[96,2048]{1,0:T(8,128)(2,1)} %get-tuple-element.9.grad) | copy-start | bytes 1179652
  61.9 0.8 %copy-start.3 = (bf16[16,16,128]{2,1,0:T(8,128)(2,1)S(1)}, bf16[16,16,128]{2,1,0:T(8,128)(2,1)}, u32[]{:S(2)}) copy-start(bf16[16,16,128]{2,1,0:T(8,128)(2,1)} %get-tuple-element.11.ig) | copy-start | bytes 196612

commit v3 on v2

--- a/solution.py
+++ b/solution.py
@@ -69,7 +69,7 @@
 
 
 MESH = pl.DeviceIdType.MESH
-CHUNK = 256
+CHUNK = 512
 BF = jnp.bfloat16
 
 
@@ -234,13 +234,14 @@
             terms[k, own_rows, cols_of(j)] = v
         t_copy(j, own_rows).start()
 
+    def add_input(j, at):
+        cols = cols_of(j)
+        y[:, at] += contract_cols(terms[1, :, cols], wg[at, cols]) + contract_cols(terms[2, :, cols], wu[at, cols])
+
     def input_sums(j):
         t_copy(j, mate_rows).wait_recv()
-        cols = cols_of(j)
-        gate_term, up_term = terms[1, :, cols], terms[2, :, cols]
         for n in range(4):
-            rows = slice(n * zw, (n + 1) * zw)
-            y[:, rows] += contract_cols(gate_term, wg[rows, cols]) + contract_cols(up_term, wu[rows, cols])
+            add_input(j, slice(n * zw, (n + 1) * zw))
 
     def tok_step(s, _):
         forward(s, 0)
@@ -250,7 +251,7 @@
     def step(s, _):
         pl.when(s < n_chunk)(lambda: forward(s, 1))
         pl.when((s >= 1) & (s < n_chunk + 1))(lambda: chip_sum(s - 1, 1))
-        pl.when((s >= 2) & (s < n_chunk + 2))(lambda: finish(s - 2))
+        pl.when(s >= 2)(lambda: finish(s - 2))
         pl.when(s >= 3)(lambda: input_sums(s - 3))
         return 0
 
@@ -258,7 +259,8 @@
     lax.fori_loop(0, n_chunk, tok_step, 0)
     chip_sum(n_chunk - 1, 0)
     out_copies.append(take(1, grad, grad_out))
-    lax.fori_loop(0, n_chunk + 3, step, 0)
+    lax.fori_loop(0, n_chunk + 2, step, 0)
+    t_copy(n_chunk - 1, mate_rows).wait_recv()
     terms_copy = pltpu.make_async_copy(terms, terms_out, o_sem.at[2])
     terms_copy.start()
 
@@ -279,6 +281,7 @@
         return pl.ds(pl.multiple_of(lax.rem(c + o, 4) * zw, zw), zw)
 
     for o in (2, 1, 3, 0):
+        add_input(n_chunk - 1, z_cols(o))
         y_snd[o] = y[row_other, z_cols(o)].astype(BF)
         y_copy(o).start()
     for o in (2, 1, 3):
@@ -439,7 +442,7 @@
             ],
             out_specs=(full(own, model), by_rows, by_rows, by_rows),
             scratch_shapes=[pltpu.VMEM((16, 16, 128), jnp.float32), pltpu.VMEM((8, model), jnp.float32)],
-            compiler_params=pltpu.CompilerParams(vmem_limit_bytes=48 * 1024 * 1024),
+            compiler_params=pltpu.CompilerParams(vmem_limit_bytes=62 * 1024 * 1024),
         )(tok, grad, terms, terms, terms, ig)
 
     return on_device

time: 73.6 us -> 64.6 us (0.88)
  Pallas kernels: 68.5 us -> 63.8 us
  local copies, waits for them, and re-layouts: 4.09 us -> 0 us
    pallas_call x1, Pallas kernels: 57.9 us -> 51.9 us  [on_device(): pl.pallas_call(functools.partial(chain_kernel, n_chunk), out_shape=(jax.S...]
    unnamed x8 -> x0, local copies, waits for them, and re-layouts: 4.09 us -> none
    pallas_call x1, Pallas kernels: 10.6 us -> 11.8 us  [on_device(): pl.pallas_call(functools.partial(grads_kernel, own, groups), grid=(width...]
where the time goes in v3:
time: 64.6 us; the launch traced here: 64.4 us
  Pallas kernels  63.8 us (99%)
    pallas_call x1, Pallas kernels, on_device(): pl.pallas_call(functools.partial(chain_kernel, n_chunk), out_shape=(jax.S...  51.9 us
    pallas_call x1, Pallas kernels, on_device(): pl.pallas_call(functools.partial(grads_kernel, own, groups), grid=(width...  11.8 us

profile of v3, /device:TPU:0, one launch (start us, length us, event | category | flops | bytes accessed | tf_op | source)
XLA Modules:
  0.0 64.4 jit_solution(16128212375260343188)
XLA Ops:
  0.6 51.9 %shard_map.102 = (bf16[96,2048]{1,0:T(8,128)(2,1)}, bf16[96,2048]{1,0:T(8,128)(2,1)}, bf16[3,96,2048]{2,1,0:T(8,128)(2,1)}, bf16[16,16,128]{2,1,0:T(8,128)(2,1)}) custom-call(bf16[12,8192]{1,0:T(8,128)(2,1)} %tok_in.1, bf16[12,8192]{1,0:T(8,128)(2,1)} %grad_in.1, bf16[2048,2048]{1,0:T(8,128)(2,1)} %wg_hbm.1, bf16[2048,2048]{1,0:T(8,128)(2,1)} %wu_hbm.1, ...), custom_call_target="tpu_custom_call" | custom-call | flops 4026531840 | bytes 25165824 | tf_op jit(solution)/shard_map/pallas_call | solution.py:374
  52.6 11.8 %shard_map.103 = (bf16[3,8192]{1,0:T(4,128)(2,1)}, bf16[2048,2048]{1,0:T(8,128)(2,1)}, bf16[2048,2048]{1,0:T(8,128)(2,1)}, bf16[2048,2048]{1,0:T(8,128)(2,1)}) custom-call(bf16[96,2048]{1,0:T(8,128)(2,1)} %get-tuple-element.8.tok, bf16[96,2048]{1,0:T(8,128)(2,1)} %get-tuple-element.9.grad, bf16[3,96,2048]{2,1,0:T(8,128)(2,1)} %get-tuple-element.10.hidden.gate_term.up_term, ...), custom_call_target="tpu_custom_call" | custom-call | tf_op jit(solution)/shard_map/pallas_call | solution.py:426

commit v4 on v3

--- a/solution.py
+++ b/solution.py
@@ -158,7 +158,8 @@
             a_copies.append(pltpu.make_async_remote_copy(
                 pk.at[a, to_d], arrived.at[a, mine, :], a_send.at[a, o], a_recv.at[a, o],
                 device_id=(to_d, to_r, c), device_id_type=MESH))
-    for cp in a_copies:
+    tok_copies, grad_copies = a_copies[:7], a_copies[7:]
+    for cp in tok_copies:
         cp.start()
     own_copies = [pltpu.make_async_copy(pk.at[a, d], arrived.at[a, mine, :], a_sem.at[a]) for a in range(2)]
     for cp in own_copies:
@@ -255,6 +256,10 @@
         pl.when(s >= 3)(lambda: input_sums(s - 3))
         return 0
 
+    for cp in tok_copies:
+        cp.wait_send()
+    for cp in grad_copies:
+        cp.start()
     out_copies = [take(0, tok, tok_out)]
     lax.fori_loop(0, n_chunk, tok_step, 0)
     chip_sum(n_chunk - 1, 0)
@@ -318,7 +323,7 @@
             device_id=(mate, r, c), device_id_type=MESH).wait_recv()
     ig_out[...] = f_rcv[...]
 
-    for cp in a_copies:
+    for cp in grad_copies:
         cp.wait_send()
 
     def drain(j, _):

time: 64.6 us -> 64.4 us (level)
  no operation moved by 1% of the time
where the time goes in v4:
time: 64.4 us; the launch traced here: 64.2 us
  Pallas kernels  63.5 us (99%)
    pallas_call x1, Pallas kernels, on_device(): pl.pallas_call(functools.partial(chain_kernel, n_chunk), out_shape=(jax.S...  51.7 us
    pallas_call x1, Pallas kernels, on_device(): pl.pallas_call(functools.partial(grads_kernel, own, groups), grid=(width...  11.8 us

profile of v4, /device:TPU:0, one launch (start us, length us, event | category | flops | bytes accessed | tf_op | source)
XLA Modules:
  0.0 64.2 jit_solution(118869915827128781)
XLA Ops:
  0.6 51.7 %shard_map.102 = (bf16[96,2048]{1,0:T(8,128)(2,1)}, bf16[96,2048]{1,0:T(8,128)(2,1)}, bf16[3,96,2048]{2,1,0:T(8,128)(2,1)}, bf16[16,16,128]{2,1,0:T(8,128)(2,1)}) custom-call(bf16[12,8192]{1,0:T(8,128)(2,1)} %tok_in.1, bf16[12,8192]{1,0:T(8,128)(2,1)} %grad_in.1, bf16[2048,2048]{1,0:T(8,128)(2,1)} %wg_hbm.1, bf16[2048,2048]{1,0:T(8,128)(2,1)} %wu_hbm.1, ...), custom_call_target="tpu_custom_call" | custom-call | flops 4026531840 | bytes 25165824 | tf_op jit(solution)/shard_map/pallas_call | solution.py:379
  52.3 11.8 %shard_map.103 = (bf16[3,8192]{1,0:T(4,128)(2,1)}, bf16[2048,2048]{1,0:T(8,128)(2,1)}, bf16[2048,2048]{1,0:T(8,128)(2,1)}, bf16[2048,2048]{1,0:T(8,128)(2,1)}) custom-call(bf16[96,2048]{1,0:T(8,128)(2,1)} %get-tuple-element.8.tok, bf16[96,2048]{1,0:T(8,128)(2,1)} %get-tuple-element.9.grad, bf16[3,96,2048]{2,1,0:T(8,128)(2,1)} %get-tuple-element.10.hidden.gate_term.up_term, ...), custom_call_target="tpu_custom_call" | custom-call | tf_op jit(solution)/shard_map/pallas_call | solution.py:431
